TPU v7x, 512 devices: a whole 4x4x16 slice. The times are simulated.
512 devices in a mesh: dp: 64 (over x_lo, z, core), tensor: 8 (over y, x_hi).
Axes of the slice: x: 4 (x_hi: 2, x_lo: 2; x = x_hi * 2 + x_lo), y: 4, z: 16, core: 2. Of those that a mesh axis runs over, the one named last changes fastest.
Arguments:
- patches: bfloat16 [14336, 6144], P('dp'), as said below
- qkv_weight: bfloat16 [6144, 3, 3072], P('dp', None, 'tensor'), as said below
- out_grad: bfloat16 [14336, 3072], P('dp', 'tensor'), may hold values from -6 to 6
- image_starts: int32 [64, 224], replicated, may hold values from -1 to 14320, as said below
Outputs:
- attended: bfloat16 [14336, 3072], P('dp', 'tensor')
- patch_grad: bfloat16 [14336, 6144], P('dp', 'tensor')
Inputs may be any that keep to these rules, and one draw needn't show every extreme that they name: `patches`: patches entries lie within -8 to 8. `qkv_weight`: entries lie within 170 / sqrt(6144) in magnitude. `image_starts`: entry (s, r) is the row of the whole packed array at which the image holding row r of shard s begins, or -1 for an empty row. On every shard the images fill rows 0 to some count without gaps, each spanning a multiple of 16 rows, and empty rows follow. For s below 64 / 2, shards s and s + 64 / 2 hold 320 image rows together; one of them holds more than 160 rows and has an image beginning at its row 160. Some shard holds 224 rows.
All inputs are finite; a program needn't handle non-finite values.
Results may differ from a plain program's by a relative error of at most 0.02.
The roundings to bfloat16 on the way count: a program that leaves them out, or rounds other values in their place, can miss the bound.
Values may be sent and summed in bfloat16 or wider, within the bound.
A program may use at most 128 MiB of HBM per device.

v0:
```python
import jax
import jax.numpy as jnp
from jax import lax
from jax.sharding import PartitionSpec as P

HD = 128


def attend(qkv_rows, image_ids, out_grad):
    score_scale = HD ** (-0.5)
    row_count = qkv_rows.shape[0]
    head_count = qkv_rows.shape[2]
    query_rows = qkv_rows[:, 0]
    key_rows = qkv_rows[:, 1]
    value_rows = qkv_rows[:, 2]
    scores = (
        jnp.einsum("qhd,khd->hqk", query_rows, key_rows, preferred_element_type=jnp.float32)
        * score_scale
    )
    allowed = (image_ids[:, None] == image_ids[None, :]) & (image_ids[None, :] >= 0)
    live_rows = (image_ids >= 0).astype(jnp.float32)
    logits = jnp.where(allowed[None], scores, -1e30)
    top_score = jnp.max(logits, axis=-1, keepdims=True)
    expo = jnp.exp(logits - top_score)
    attn_probs = expo / jnp.sum(expo, axis=-1, keepdims=True) * live_rows[None, :, None]
    probs_low = attn_probs.astype(jnp.bfloat16)
    attended = jnp.einsum(
        "hqk,khd->qhd", probs_low, value_rows, preferred_element_type=jnp.float32
    ).astype(jnp.bfloat16)
    grad_out = out_grad.reshape(row_count, head_count, HD)
    grad_probs = jnp.einsum(
        "qhd,khd->hqk", grad_out, value_rows, preferred_element_type=jnp.float32
    )
    grad_value = jnp.einsum(
        "hqk,qhd->khd", probs_low, grad_out, preferred_element_type=jnp.float32
    ).astype(jnp.bfloat16)
    row_delta = jnp.sum(attn_probs * grad_probs, axis=-1, keepdims=True)
    grad_scores = (attn_probs * (grad_probs - row_delta) * score_scale).astype(jnp.bfloat16)
    grad_query = jnp.einsum(
        "hqk,khd->qhd", grad_scores, key_rows, preferred_element_type=jnp.float32
    ).astype(jnp.bfloat16)
    grad_key = jnp.einsum(
        "hqk,qhd->khd", grad_scores, query_rows, preferred_element_type=jnp.float32
    ).astype(jnp.bfloat16)
    grad_qkv = jnp.stack([grad_query, grad_key, grad_value], axis=1)
    return (
        attended.reshape(row_count, head_count * HD),
        grad_qkv.reshape(row_count, 3, head_count * HD),
    )


def project(rows, image_ids, grads, weight):
    columns = weight.shape[1] * weight.shape[2]
    flat_weight = weight.reshape(weight.shape[0], columns)
    qkv_rows = jnp.dot(rows, flat_weight, preferred_element_type=jnp.float32).astype(jnp.bfloat16)
    qkv_rows = qkv_rows.reshape(rows.shape[0], 3, weight.shape[2] // HD, HD)
    attended, grad_qkv = attend(qkv_rows, image_ids, grads)
    partial_value = lax.dot_general(
        grad_qkv.reshape(rows.shape[0], columns),
        flat_weight,
        (((1,), (1,)), ((), ())),
        preferred_element_type=jnp.float32,
    )
    return (attended, partial_value)


def local(patches, qkv_weight, out_grad, image_starts):
    weight = lax.all_gather(qkv_weight, "dp", axis=0, tiled=True)
    dp_index = lax.axis_index("dp")
    own_ids = lax.dynamic_index_in_dim(image_starts, dp_index, 0, keepdims=False)
    attended, partial_value = project(patches, own_ids, out_grad, weight)
    patch_grad = lax.psum_scatter(
        partial_value.astype(jnp.bfloat16), "tensor", scatter_dimension=1, tiled=True
    )
    return (attended, patch_grad)


def solution(mesh):
    in_specs = (P("dp", None), P("dp", None, "tensor"), P("dp", "tensor"), P())
    out_specs = (P("dp", "tensor"), P("dp", "tensor"))
    return jax.shard_map(local, mesh=mesh, in_specs=in_specs, out_specs=out_specs, check_vma=False)
```

profile of v0, /device:TPU:1, one launch (start us, length us, event | category | flops | bytes accessed | tf_op | source)
XLA Modules:
  0.0 300.1 jit_solution(10452343615732673158)
XLA Ops:
  7.2 0.0 copy-start
  7.2 0.0 all-gather.2.cloned.1.call-start
  7.2 0.7 all-gather.2.cloned.1.call-update
  7.9 0.0 reduce-scatter.2.cloned.1.call-start
  8.0 1.1 copy.33
  9.1 0.7 compare_reduce_fusion
  9.8 0.7 compare_and_fusion
  10.5 142.5 %all-gather.2.cloned.1.call-done = bf16[6144,3,384]{2,0,1:T(8,128)(2,1)} async-done(((bf16[96,3,384]{2,0,1:T(8,128)(2,1)}), bf16[6144,3,384]{2,0,1:T(8,128)(2,1)}) %all-gather.2.cloned.1.call-update) | async-done | bytes 14155792 | tf_op jit(solution)/shard_map/all_gather | solution.py:68
  153.0 18.6 %copy.26 = bf16[6144,3,384]{0,2,1:T(8,128)(2,1)} copy(bf16[6144,3,384]{2,0,1:T(8,128)(2,1)} %all-gather.2.cloned.1.call-done) | data formatting | bytes 28311552 | tf_op jit(solution)/shard_map/all_gather | solution.py:68
  171.6 0.0 copy-done
  171.7 8.6 %convolution_convert_fusion.1 = bf16[224,1152]{1,0:T(8,128)(2,1)} fusion(bf16[224,6144]{1,0:T(8,128)(2,1)S(1)} %copy-done, bf16[6144,1152]{0,1:T(8,128)(2,1)} %bitcast.74), kind=kOutput, calls=%fused_computation.3 | convolution fusion | flops 3171151872 | bytes 17424384 | tf_op jit(solution)/shard_map/dot_general | solution.py:55
  180.2 1.3 copy.27
  181.5 0.0 copy-start.1
  181.5 2.1 fusion.28
  183.6 1.1 convolution_bitcast_fusion
  184.8 2.0 fusion.11
  186.8 2.1 fusion.12
  188.9 2.9 fusion.10
  191.8 0.0 copy-done.1
  191.8 1.8 pad_maximum_fusion
  193.6 1.3 copy.37
  194.9 10.3 %convolution_convert_fusion = bf16[224,6144]{1,0:T(8,128)(2,1)} fusion(bf16[224,1152]{0,1:T(8,128)(2,1)S(1)} %bitcast.76, bf16[6144,1152]{0,1:T(8,128)(2,1)} %bitcast.75), kind=kOutput, calls=%fused_computation.2 | convolution fusion | flops 3172270080 | bytes 17424384 | tf_op jit(solution)/shard_map/dot_general | solution.py:58
  205.2 0.0 reduce-scatter.2.cloned.1.call-update
  205.2 1.8 fusion.9
  207.0 0.1 copy.32
  207.2 0.8 copy.38
  208.0 85.3 %reduce-scatter.2.cloned.1.call-done = bf16[224,768]{1,0:T(8,128)(2,1)} async-done(((bf16[224,6144]{1,0:T(8,128)(2,1)}), bf16[224,768]{1,0:T(8,128)(2,1)}) %reduce-scatter.2.cloned.1.call-update) | async-done | bytes 344080 | tf_op jit(solution)/shard_map/reduce_scatter | solution.py:72
  (1 shorter events, 0.0 us)
Async XLA Ops:
  7.2 164.5 %copy-start = (bf16[224,6144]{1,0:T(8,128)(2,1)S(1)}, bf16[224,6144]{1,0:T(8,128)(2,1)}, u32[]{:S(2)}) copy-start(bf16[224,6144]{1,0:T(8,128)(2,1)} %param.4) | copy-start | bytes 8257540
  7.2 145.9 %all-gather.2.cloned.1.call-start = ((), (), s32[]{:S(2)}) async-start(), calls=%async_computation.1 | async-start | bytes 14376960 | tf_op jit(solution)/shard_map/all_gather | solution.py:68
  7.9 285.3 %reduce-scatter.2.cloned.1.call-start = ((), (), s32[]{:S(2)}) async-start(), calls=%async_computation.2 | async-start | bytes 3096576 | tf_op jit(solution)/shard_map/reduce_scatter | solution.py:72
  181.5 10.3 %copy-start.1 = (bf16[224,1152]{0,1:T(8,128)(2,1)}, bf16[224,1152]{0,1:T(8,128)(2,1)S(1)}, u32[]{:S(2)}) copy-start(bf16[224,1152]{0,1:T(8,128)(2,1)S(1)} %copy.27) | copy-start | bytes 1548292
Sparse Core Ops, SparseCore 0:
  10.1 142.8 all-gather.1
  205.3 87.8 reduce-scatter.1
where the time goes:
time: 301 us; the launch traced here: 300 us
  waiting for transfers between devices  229 us (76%)
  matrix products  30.9 us (10%)
  local copies, waits for them, and re-layouts  23.2 us (8%)
  between operations  14.1 us (5%)
  other arithmetic  3.31 us (1%)
    all_gather x1, waiting for transfers between devices, local(): weight = lax.all_gather(qkv_weight, 'dp', axis=0, tiled=True)  143 us
    reduce_scatter x1, waiting for transfers between devices, local(): lax.psum_scatter(partial_value.astype(jnp.bfloat16), 'tensor', scatter_di...  85.3 us
    all_gather x1, local copies, waits for them, and re-layouts, local(): weight = lax.all_gather(qkv_weight, 'dp', axis=0, tiled=True)  18.6 us
    dot_general x1, matrix products, project(): lax.dot_general(grad_qkv.reshape(rows.shape[0], columns), flat_weight, ((...  10.3 us
    dot_general x1, matrix products, project(): jnp.dot(rows, flat_weight, preferred_element_type=jnp.float32)  8.58 us
  transfers between devices with their start and end apart: 2, of which 2 were waited for; matrix products, arithmetic and copies ran while one was open for 2% of the time, Pallas kernels for 0%

commit v1 on v0

v1 whole, which is shorter than its diff:
```python
import functools

import jax
import jax.numpy as jnp
from jax import lax
from jax.experimental import pallas as pl
from jax.experimental.pallas import tpu as pltpu
from jax.sharding import PartitionSpec as P

HD = 128
NZ = 16
NY = 4
MESH = pl.DeviceIdType.MESH
PIECE = 384


def attend_head(query, key, value, grad_out, allowed, live):
    score_scale = HD ** (-0.5)
    nt = (((1,), (1,)), ((), ()))
    tn = (((0,), (0,)), ((), ()))
    scores = lax.dot_general(query, key, nt, preferred_element_type=jnp.float32) * score_scale
    logits = jnp.where(allowed, scores, -1e30)
    top_score = jnp.max(logits, axis=-1, keepdims=True)
    expo = jnp.exp(logits - top_score)
    probs = expo / jnp.sum(expo, axis=-1, keepdims=True) * live
    low = probs.astype(jnp.bfloat16)
    attended = jnp.dot(low, value, preferred_element_type=jnp.float32).astype(jnp.bfloat16)
    grad_probs = lax.dot_general(grad_out, value, nt, preferred_element_type=jnp.float32)
    grad_value = lax.dot_general(low, grad_out, tn, preferred_element_type=jnp.float32).astype(jnp.bfloat16)
    row_delta = jnp.sum(probs * grad_probs, axis=-1, keepdims=True)
    grad_scores = (probs * (grad_probs - row_delta) * score_scale).astype(jnp.bfloat16)
    grad_query = jnp.dot(grad_scores, key, preferred_element_type=jnp.float32).astype(jnp.bfloat16)
    grad_key = lax.dot_general(grad_scores, query, tn, preferred_element_type=jnp.float32).astype(jnp.bfloat16)
    return attended, grad_query, grad_key, grad_value


def kernel(
    x_ref, w_ref, g_ref, idc_ref, idr_ref, att_ref, out_ref,
    wbuf, acc, qkv, gbuf, sbuf, rbuf, zs, zr, xs, xr, cs, cr, ts, tr,
):
    dp, t = lax.axis_index("dp"), lax.axis_index("tensor")
    xl, z, c = dp // (2 * NZ), (dp // 2) % NZ, dp % 2
    y, xh = t // 2, t % 2
    heads = w_ref.shape[1] // (3 * HD)
    width = heads * HD

    def dev(xl_, z_, c_):
        return (xl_ * (2 * NZ) + z_ * 2 + c_, t)

    z_next = (dev(xl, (z + 1) % NZ, c), dev(xl, (z + NZ - 1) % NZ, c))
    x_dev = dev(1 - xl, z, c)
    c_dev = dev(xl, z, 1 - c)
    peers = [(dp, ((y + j // 2) % NY) * 2 + (xh + j) % 2) for j in range(1, 8)]

    barrier = pltpu.get_barrier_semaphore()
    everyone = [*z_next, x_dev, c_dev, *peers]
    for other in everyone:
        pl.semaphore_signal(barrier, inc=1, device_id=other, device_id_type=MESH)
    pl.semaphore_wait(barrier, len(everyone))

    def origin(d, s):
        return (z - s + NZ) % NZ if d == 0 else (z + s) % NZ

    def part(xl_, z_, c_, p):
        return wbuf.at[xl_ * (2 * NZ) + z_ * 2 + c_, :, p * PIECE : (p + 1) * PIECE]

    def whole(xl_, z_, c_):
        return wbuf.at[xl_ * (2 * NZ) + z_ * 2 + c_]

    def z_ref(zo, p):
        return part(1 - xl, zo, c, 0) if p == 0 else part(xl, zo, c, p - 1)

    def remote(ref, send, recv, device):
        return pltpu.make_async_remote_copy(
            src_ref=ref, dst_ref=ref, send_sem=send, recv_sem=recv, device_id=device, device_id_type=MESH
        )

    def z_send(d, s, p):
        return remote(z_ref(origin(d, s - 1), p), zs.at[d, s, p], zr.at[d, s, p], z_next[d])

    def z_recv(d, s, p):
        return remote(z_ref(origin(d, s), p), zs.at[d, s, p], zr.at[d, s, p], z_next[d])

    def x_send(d, s, p):
        return remote(part(xl, origin(d, s), c, p), xs.at[d, s, p], xr.at[d, s, p], x_dev)

    def x_recv(d, s, p):
        return remote(part(1 - xl, origin(d, s), c, p), xs.at[d, s, p], xr.at[d, s, p], x_dev)

    def c_send(d, s, k):
        return remote(whole((xl + k) % 2, origin(d, s), c), cs.at[d, s, k], cr.at[d, s, k], c_dev)

    def c_recv(d, s, k):
        return remote(whole((xl + k) % 2, origin(d, s), 1 - c), cs.at[d, s, k], cr.at[d, s, k], c_dev)

    def multiply(s):
        zc = jnp.where((z + s) % 2 == 1, (z + s) % NZ, (z - s + NZ) % NZ) // 2
        for half in range(2):
            unit = half * (NZ // 2) + zc
            rows = wbuf[pl.ds(unit * 4, 4)].reshape(4 * w_ref.shape[0], w_ref.shape[1])
            cols = pl.ds(pl.multiple_of(unit * (4 * w_ref.shape[0]), 128), 4 * w_ref.shape[0])
            acc[...] += jnp.dot(x_ref[:, cols], rows, preferred_element_type=jnp.float32)

    wbuf[xl * (2 * NZ) + z * 2 + c] = w_ref[...]
    for p in range(3):
        x_send(0, 0, p).start()
    for p in range(1, 4):
        for d in range(2):
            z_send(d, 1, p).start()
    c_send(0, 0, 0).start()
    acc[...] = jnp.zeros_like(acc)
    x_recv(0, 0, 0).wait_recv()
    for d in range(2):
        z_send(d, 1, 0).start()
    x_recv(0, 0, 1).wait_recv()
    x_recv(0, 0, 2).wait_recv()
    c_send(0, 0, 1).start()

    order = (1, 2, 3, 0)
    last = {0: 0, 1: 0, 2: 1, 3: 1}

    def step(s, carry):
        for p in order:
            for d in range(2):
                z_recv(d, s, p).wait_recv()
                if last[p] == d:
                    z_send(d, s + 1, p).start()
                else:
                    @pl.when(s < NZ // 2 - 1)
                    def _():
                        z_send(d, s + 1, p).start()
                if p >= 2:
                    x_send(d, s, p - 1).start()
        for d in range(2):
            c_send(d, s, 0).start()

        @pl.when(s == 1)
        def _():
            for k in range(2):
                c_recv(0, 0, k).wait_recv()

        @pl.when(s > 1)
        def _():
            for d in range(2):
                for k in range(2):
                    c_recv(d, s - 1, k).wait_recv()
            multiply(s - 1)

        for d in range(2):
            x_recv(d, s, 1).wait_recv()
            x_recv(d, s, 2).wait_recv()
            c_send(d, s, 1).start()
        return carry

    lax.fori_loop(1, NZ // 2, step, 0)
    far = NZ // 2
    for p in order:
        z_recv(last[p], far, p).wait_recv()
        if p >= 2:
            x_send(0, far, p - 1).start()
    c_send(0, far, 0).start()
    for d in range(2):
        for k in range(2):
            c_recv(d, far - 1, k).wait_recv()
    multiply(far - 1)
    x_recv(0, far, 1).wait_recv()
    x_recv(0, far, 2).wait_recv()
    c_send(0, far, 1).start()
    for k in range(2):
        c_recv(0, far, k).wait_recv()
    multiply(far)

    qkv[...] = acc[...].astype(jnp.bfloat16)
    allowed = (idc_ref[...] == idr_ref[...]) & (idr_ref[...] >= 0)
    live = (idc_ref[...] >= 0).astype(jnp.float32)
    for h in range(heads):
        at = [slice(i * width + h * HD, i * width + (h + 1) * HD) for i in range(3)]
        attended, *grads = attend_head(
            qkv[:, at[0]], qkv[:, at[1]], qkv[:, at[2]], g_ref[:, h * HD : (h + 1) * HD], allowed, live
        )
        att_ref[:, h * HD : (h + 1) * HD] = attended
        for i in range(3):
            gbuf[:, at[i]] = grads[i]

    blocks = wbuf.shape[0] // 8
    depth = blocks * w_ref.shape[0]

    def dest(i):
        k = i // 2
        dy = jnp.where(k < 2, k + 2, 3 - k)
        return ((y + dy) % NY) * 2 + (xh + 1 - i % 2) % 2

    def source_free(i):
        return pltpu.make_async_remote_copy(
            src_ref=sbuf.at[i], dst_ref=rbuf.at[i], send_sem=ts.at[i], recv_sem=tr.at[i],
            device_id=(dp, dest(i)), device_id_type=MESH,
        )

    def backward(i, carry):
        rows = wbuf[pl.ds(dest(i) * blocks, blocks)].reshape(depth, w_ref.shape[1])
        sbuf[i] = lax.dot_general(
            gbuf[...], rows, (((1,), (1,)), ((), ())), preferred_element_type=jnp.float32
        ).astype(jnp.bfloat16)

        @pl.when(i < 7)
        def _():
            source_free(i).start()

        return carry

    lax.fori_loop(0, 8, backward, 0)

    for p in range(3):
        x_send(0, 0, p).wait_send()
    for k in range(2):
        c_send(0, 0, k).wait_send()

    def drain(s, carry):
        for d in range(2):
            for p in range(4):
                z_send(d, s, p).wait_send()
            for p in (1, 2):
                x_send(d, s, p).wait_send()
            for k in range(2):
                c_send(d, s, k).wait_send()
        return carry

    lax.fori_loop(1, NZ // 2, drain, 0)
    for p in range(4):
        z_send(last[p], far, p).wait_send()
    for p in (1, 2):
        x_send(0, far, p).wait_send()
    for k in range(2):
        c_send(0, far, k).wait_send()

    total = sbuf[7].astype(jnp.float32)
    for i in range(7):
        source_free(i).wait_recv()
        total += rbuf[i].astype(jnp.float32)
    out_ref[...] = total.astype(jnp.bfloat16)
    for i in range(7):
        source_free(i).wait_send()


def local(patches, qkv_weight, out_grad, image_starts):
    rows, model = patches.shape
    share = qkv_weight.shape[0]
    columns = qkv_weight.shape[1] * qkv_weight.shape[2]
    n_dp = model // share
    ids = lax.dynamic_index_in_dim(image_starts, lax.axis_index("dp"), 0, keepdims=False)
    vmem = pl.BlockSpec(memory_space=pltpu.VMEM)
    bf = jnp.bfloat16
    dma = pltpu.SemaphoreType.DMA
    steps = NZ // 2 + 1
    return pl.pallas_call(
        kernel,
        out_shape=(
            jax.ShapeDtypeStruct(out_grad.shape, bf),
            jax.ShapeDtypeStruct((rows, model // 8), bf),
        ),
        in_specs=[vmem] * 5,
        out_specs=(vmem, vmem),
        scratch_shapes=[
            pltpu.VMEM((n_dp, share, columns), bf),
            pltpu.VMEM((rows, columns), jnp.float32),
            pltpu.VMEM((rows, columns), bf),
            pltpu.VMEM((rows, columns), bf),
            pltpu.VMEM((8, rows, model // 8), bf),
            pltpu.VMEM((7, rows, model // 8), bf),
            dma((2, steps, 4)),
            dma((2, steps, 4)),
            dma((2, steps, 3)),
            dma((2, steps, 3)),
            dma((2, steps, 2)),
            dma((2, steps, 2)),
            dma((8,)),
            dma((8,)),
        ],
        compiler_params=pltpu.CompilerParams(
            collective_id=0, has_side_effects=True, vmem_limit_bytes=56 * 1024 * 1024
        ),
    )(patches, qkv_weight.reshape(share, columns), out_grad, ids[:, None], ids[None, :])


def solution(mesh):
    in_specs = (P("dp", None), P("dp", None, "tensor"), P("dp", "tensor"), P())
    out_specs = (P("dp", "tensor"), P("dp", "tensor"))
    return jax.shard_map(local, mesh=mesh, in_specs=in_specs, out_specs=out_specs, check_vma=False)
```

time: 301 us -> 124 us (0.41)
  waiting for transfers between devices: 229 us -> 0 us
  Pallas kernels: 0 us -> 116 us
  matrix products: 30.9 us -> 0 us
  local copies, waits for them, and re-layouts: 23.2 us -> 7.18 us
  between operations: 14.1 us -> 0.65 us
  other arithmetic: 3.31 us -> 0 us
    all_gather x1 -> x0, waiting for transfers between devices: 143 us -> none  [local(): weight = lax.all_gather(qkv_weight, 'dp', axis=0, tiled=True)]
    pallas_call x0 -> x1, Pallas kernels: none -> 116 us  [local(): pl.pallas_call(kernel, out_shape=(jax.ShapeDtypeStruct(out_grad.shape, bf...]
    reduce_scatter x1 -> x0, waiting for transfers between devices: 85.3 us -> none  [local(): lax.psum_scatter(partial_value.astype(jnp.bfloat16), 'tensor', scatter_di...]
    dot_general x7 -> x0, matrix products: 28.8 us -> none  [the longest x1 10.3 us: project(): lax.dot_general(grad_qkv.reshape(rows.shape[0], columns), flat_weight, ((...]
    all_gather x1 -> x0, local copies, waits for them, and re-layouts: 18.6 us -> none  [local(): weight = lax.all_gather(qkv_weight, 'dp', axis=0, tiled=True)]
  transfers between devices with their start and end apart: 2 -> 0, of which waited for: 2 -> 0; matrix products, arithmetic and copies ran while one was open for 2% -> 0% of each run, Pallas kernels for 0% -> 0%
where the time goes in v1:
time: 124 us
  Pallas kernels  116 us (94%)
  local copies, waits for them, and re-layouts  7.18 us (6%)
    pallas_call x1, Pallas kernels, local(): pl.pallas_call(kernel, out_shape=(jax.ShapeDtypeStruct(out_grad.shape, bf...  116 us
    unnamed x4, local copies, waits for them, and re-layouts  4.17 us

profile of v1, /device:TPU:1, one launch (start us, length us, event | category | flops | bytes accessed | tf_op | source)
XLA Modules:
  0.0 123.9 jit_solution(15140530938251802598)
XLA Ops:
  0.6 0.0 copy-start
  0.6 0.8 copy-done
  1.5 0.6 constant_dynamic-slice_fusion.idr_ref
  2.1 0.8 copy.8.idc_ref
  2.8 1.6 %copy.9 = bf16[3,12,8,384]{3,2,0,1:T(8,128)(2,1)} copy(bf16[3,12,8,384]{3,2,1,0:T(8,128)(2,1)} %bitcast.5) | data formatting | bytes 442368 | tf_op jit(solution)/shard_map/reshape | solution.py:282
  4.5 116.1 %shard_map.59 = (bf16[224,384]{1,0:T(8,128)(2,1)}, bf16[224,768]{1,0:T(8,128)(2,1)}) custom-call(bf16[224,6144]{1,0:T(8,128)(2,1)} %x_ref.1, bf16[96,1152]{1,0:T(8,128)(2,1)} %bitcast.4, bf16[224,384]{1,0:T(8,128)(2,1)} %g_ref.1, s32[224,1]{1,0:T(8,128)} %copy.8.idc_ref, s32[1,224]{1,0:T(1,128)} %constant_dynamic-slice_fusion.idr_ref), custom_call_target="tpu_custom_call" | custom-call | tf_op jit(solution)/shard_map/pallas_call | solution.py:255
  120.6 1.6 %copy.12 = bf16[224,384]{1,0:T(8,128)(2,1)} copy(bf16[224,384]{1,0:T(8,128)(2,1)} %get-tuple-element.4) | data formatting | bytes 344064
  122.2 1.7 %copy.13 = bf16[224,768]{1,0:T(8,128)(2,1)} copy(bf16[224,768]{1,0:T(8,128)(2,1)} %get-tuple-element.5) | data formatting | bytes 688128
  (1 shorter events, 0.0 us)
Async XLA Ops:
  0.6 0.8 copy-start

commit v2 on v1

--- a/solution.py
+++ b/solution.py
@@ -10,8 +10,11 @@
 HD = 128
 NZ = 16
 NY = 4
+UNIT = 16
+CAP = 160
+MOVE = 64
+BASE = CAP - MOVE
 MESH = pl.DeviceIdType.MESH
-PIECE = 384
 
 
 def attend_head(query, key, value, grad_out, allowed, live):
@@ -34,15 +37,32 @@
     return attended, grad_query, grad_key, grad_value
 
 
+def column(ids_ref, shard):
+    row = ids_ref[pl.ds(shard, 1), :].astype(jnp.float32)
+    return jnp.broadcast_to(row, (HD, row.shape[1])).T
+
+
+def units(rows, first):
+    return [rows[first + at : first + at + UNIT] for at in range(0, MOVE, UNIT)]
+
+
+def pick(mask, there, other):
+    kept = jnp.where(mask, there.astype(jnp.float32), other.astype(jnp.float32) if other is not None else 0.0)
+    return kept.astype(there.dtype)
+
+
 def kernel(
-    x_ref, w_ref, g_ref, idc_ref, idr_ref, att_ref, out_ref,
-    wbuf, acc, qkv, gbuf, sbuf, rbuf, zs, zr, xs, xr, cs, cr, ts, tr,
+    x_ref, w_ref, g_ref, ids_ref, att_ref, out_ref,
+    wbuf, acc, qkv, gbuf, sbuf, rbuf, xw, mbuf, gw, gm, attw, am, outw, om,
+    zs, zr, xs, xr, cs, cr, ts, tr, ms, mr, ps, pr, lsem,
 ):
     dp, t = lax.axis_index("dp"), lax.axis_index("tensor")
     xl, z, c = dp // (2 * NZ), (dp // 2) % NZ, dp % 2
     y, xh = t // 2, t % 2
-    heads = w_ref.shape[1] // (3 * HD)
-    width = heads * HD
+    share, width = w_ref.shape[1:]
+    slot = g_ref.shape[0]
+    quarter = xw.shape[1] // NY
+    heads = width // HD
 
     def dev(xl_, z_, c_):
         return (xl_ * (2 * NZ) + z_ * 2 + c_, t)
@@ -50,10 +70,11 @@
     z_next = (dev(xl, (z + 1) % NZ, c), dev(xl, (z + NZ - 1) % NZ, c))
     x_dev = dev(1 - xl, z, c)
     c_dev = dev(xl, z, 1 - c)
+    cross = (dev(1 - xl, z, c)[0], y * 2 + 1 - xh)
     peers = [(dp, ((y + j // 2) % NY) * 2 + (xh + j) % 2) for j in range(1, 8)]
 
     barrier = pltpu.get_barrier_semaphore()
-    everyone = [*z_next, x_dev, c_dev, *peers]
+    everyone = [*z_next, x_dev, c_dev, cross, *peers]
     for other in everyone:
         pl.semaphore_signal(barrier, inc=1, device_id=other, device_id_type=MESH)
     pl.semaphore_wait(barrier, len(everyone))
@@ -62,7 +83,7 @@
         return (z - s + NZ) % NZ if d == 0 else (z + s) % NZ
 
     def part(xl_, z_, c_, p):
-        return wbuf.at[xl_ * (2 * NZ) + z_ * 2 + c_, :, p * PIECE : (p + 1) * PIECE]
+        return wbuf.at[xl_ * (2 * NZ) + z_ * 2 + c_, p]
 
     def whole(xl_, z_, c_):
         return wbuf.at[xl_ * (2 * NZ) + z_ * 2 + c_]
@@ -92,15 +113,44 @@
 
     def c_recv(d, s, k):
         return remote(whole((xl + k) % 2, origin(d, s), 1 - c), cs.at[d, s, k], cr.at[d, s, k], c_dev)
+
+    def weight_rows(first, count):
+        return jnp.concatenate(
+            [wbuf[pl.ds(first, count), p].reshape(count * share, width) for p in range(3)], axis=1
+        )
 
     def multiply(s):
         zc = jnp.where((z + s) % 2 == 1, (z + s) % NZ, (z - s + NZ) % NZ) // 2
         for half in range(2):
             unit = half * (NZ // 2) + zc
-            rows = wbuf[pl.ds(unit * 4, 4)].reshape(4 * w_ref.shape[0], w_ref.shape[1])
-            cols = pl.ds(pl.multiple_of(unit * (4 * w_ref.shape[0]), 128), 4 * w_ref.shape[0])
-            acc[...] += jnp.dot(x_ref[:, cols], rows, preferred_element_type=jnp.float32)
-
+            cols = pl.ds(pl.multiple_of(unit * (4 * share), 128), 4 * share)
+            acc[...] += jnp.dot(xw[:, cols], weight_rows(unit * 4, 4), preferred_element_type=jnp.float32)
+
+    def move_copy(k, quarter_at, device):
+        ref = mbuf.at[quarter_at]
+        cols = pl.ds(pl.multiple_of(y * quarter, HD), quarter)
+        src = x_ref.at[pl.ds(CAP, MOVE), cols] if k == 0 else ref
+        return pltpu.make_async_remote_copy(
+            src_ref=src, dst_ref=ref, send_sem=ms.at[k], recv_sem=mr.at[k], device_id=device, device_id_type=MESH
+        )
+
+    def move_send(k):
+        return move_copy(k, y, cross if k == 0 else (dp, ((y + k) % NY) * 2 + xh))
+
+    def move_recv(k):
+        return move_copy(k, (y - k + NY) % NY, cross)
+
+    def swap(k, src, dst):
+        return pltpu.make_async_remote_copy(
+            src_ref=src, dst_ref=dst, send_sem=ps.at[k], recv_sem=pr.at[k], device_id=x_dev, device_id_type=MESH
+        )
+
+    grads_swap = swap(0, g_ref.at[pl.ds(CAP, MOVE)], gm)
+    att_swap = swap(1, attw.at[pl.ds(BASE, MOVE)], am)
+    out_swap = swap(2, outw, om)
+    own_rows = pltpu.make_async_copy(x_ref.at[pl.ds(0, CAP)], xw, lsem)
+
+    own_rows.start()
     wbuf[xl * (2 * NZ) + z * 2 + c] = w_ref[...]
     for p in range(3):
         x_send(0, 0, p).start()
@@ -108,7 +158,29 @@
         for d in range(2):
             z_send(d, 1, p).start()
     c_send(0, 0, 0).start()
+    move_send(0).start()
     acc[...] = jnp.zeros_like(acc)
+    own_ids = column(ids_ref, dp)
+    other_ids = column(ids_ref, dev(1 - xl, z, c)[0])
+    own_live = own_ids[:, :1] >= 0.0
+    taken = [
+        jnp.where(own >= 0.0, own, other)
+        for own, other in zip(units(own_ids, BASE), units(other_ids, CAP)[::-1], strict=True)
+    ]
+    work_ids = jnp.concatenate([own_ids[:BASE], *taken], axis=0)
+
+    def fill():
+        for k in range(1, NY):
+            move_recv(k).wait_recv()
+        own_rows.wait()
+        for at in range(MOVE // UNIT):
+            mask = own_live[BASE + at * UNIT : BASE + (at + 1) * UNIT]
+            rows = pl.ds(BASE + at * UNIT, UNIT)
+            back = pl.ds(MOVE - (at + 1) * UNIT, UNIT)
+            for q in range(NY):
+                cols = pl.ds(q * quarter, quarter)
+                xw[rows, cols] = pick(mask, xw[rows, cols], mbuf[q, back, :])
+
     x_recv(0, 0, 0).wait_recv()
     for d in range(2):
         z_send(d, 1, 0).start()
@@ -116,8 +188,20 @@
     x_recv(0, 0, 2).wait_recv()
     c_send(0, 0, 1).start()
 
-    order = (1, 2, 3, 0)
+    order = (2, 3, 1, 0)
     last = {0: 0, 1: 0, 2: 1, 3: 1}
+    far = NZ // 2
+
+    def pass_x(d, s):
+        x_recv(d, s, 1).wait_recv()
+        x_recv(d, s, 2).wait_recv()
+        c_send(d, s, 1).start()
+
+    def use(ds, s):
+        for d in ds:
+            for k in range(2):
+                c_recv(d, s, k).wait_recv()
+        multiply(s)
 
     def step(s, carry):
         for p in order:
@@ -126,7 +210,7 @@
                 if last[p] == d:
                     z_send(d, s + 1, p).start()
                 else:
-                    @pl.when(s < NZ // 2 - 1)
+                    @pl.when(s < far - 1)
                     def _():
                         z_send(d, s + 1, p).start()
                 if p >= 2:
@@ -138,77 +222,94 @@
         def _():
             for k in range(2):
                 c_recv(0, 0, k).wait_recv()
+            move_recv(0).wait_recv()
+            for k in range(1, NY):
+                move_send(k).start()
+            grads_swap.start()
 
         @pl.when(s > 1)
         def _():
             for d in range(2):
-                for k in range(2):
-                    c_recv(d, s - 1, k).wait_recv()
-            multiply(s - 1)
-
-        for d in range(2):
-            x_recv(d, s, 1).wait_recv()
-            x_recv(d, s, 2).wait_recv()
-            c_send(d, s, 1).start()
+                pass_x(d, s - 1)
+
+        @pl.when(s == 3)
+        def _():
+            fill()
+
+        @pl.when(s > 2)
+        def _():
+            use((0, 1), s - 2)
+
         return carry
 
-    lax.fori_loop(1, NZ // 2, step, 0)
-    far = NZ // 2
+    lax.fori_loop(1, far, step, 0)
     for p in order:
         z_recv(last[p], far, p).wait_recv()
         if p >= 2:
             x_send(0, far, p - 1).start()
     c_send(0, far, 0).start()
     for d in range(2):
-        for k in range(2):
-            c_recv(d, far - 1, k).wait_recv()
-    multiply(far - 1)
-    x_recv(0, far, 1).wait_recv()
-    x_recv(0, far, 2).wait_recv()
-    c_send(0, far, 1).start()
-    for k in range(2):
-        c_recv(0, far, k).wait_recv()
-    multiply(far)
+        pass_x(d, far - 1)
+    use((0, 1), far - 2)
+    pass_x(0, far)
+    use((0, 1), far - 1)
+    use((0,), far)
 
     qkv[...] = acc[...].astype(jnp.bfloat16)
-    allowed = (idc_ref[...] == idr_ref[...]) & (idr_ref[...] >= 0)
-    live = (idc_ref[...] >= 0).astype(jnp.float32)
+    row_ids = work_ids.T[:1]
+    allowed = (work_ids[:, :1] == row_ids) & (row_ids >= 0.0)
+    live = (work_ids[:, :1] >= 0.0).astype(jnp.float32)
+    grads_swap.wait_recv()
+    gw[pl.ds(0, BASE)] = g_ref[pl.ds(0, BASE)]
+    for at in range(MOVE // UNIT):
+        rows = pl.ds(BASE + at * UNIT, UNIT)
+        mask = own_live[BASE + at * UNIT : BASE + (at + 1) * UNIT]
+        gw[rows] = pick(mask, g_ref[rows], gm[pl.ds(MOVE - (at + 1) * UNIT, UNIT)])
     for h in range(heads):
         at = [slice(i * width + h * HD, i * width + (h + 1) * HD) for i in range(3)]
         attended, *grads = attend_head(
-            qkv[:, at[0]], qkv[:, at[1]], qkv[:, at[2]], g_ref[:, h * HD : (h + 1) * HD], allowed, live
-        )
-        att_ref[:, h * HD : (h + 1) * HD] = attended
+            qkv[:, at[0]], qkv[:, at[1]], qkv[:, at[2]], gw[:, h * HD : (h + 1) * HD], allowed, live
+        )
+        attw[:, h * HD : (h + 1) * HD] = attended
         for i in range(3):
             gbuf[:, at[i]] = grads[i]
 
+    att_swap.start()
+
     blocks = wbuf.shape[0] // 8
-    depth = blocks * w_ref.shape[0]
 
     def dest(i):
         k = i // 2
         dy = jnp.where(k < 2, k + 2, 3 - k)
         return ((y + dy) % NY) * 2 + (xh + 1 - i % 2) % 2
 
-    def source_free(i):
+    parts = (pl.ds(BASE, MOVE), pl.ds(0, BASE))
+
+    def sums(i, b):
         return pltpu.make_async_remote_copy(
-            src_ref=sbuf.at[i], dst_ref=rbuf.at[i], send_sem=ts.at[i], recv_sem=tr.at[i],
+            src_ref=sbuf.at[i, parts[b]], dst_ref=rbuf.at[i, parts[b]], send_sem=ts.at[b, i], recv_sem=tr.at[b, i],
             device_id=(dp, dest(i)), device_id_type=MESH,
         )
 
     def backward(i, carry):
-        rows = wbuf[pl.ds(dest(i) * blocks, blocks)].reshape(depth, w_ref.shape[1])
+        rows = weight_rows(dest(i) * blocks, blocks)
         sbuf[i] = lax.dot_general(
             gbuf[...], rows, (((1,), (1,)), ((), ())), preferred_element_type=jnp.float32
         ).astype(jnp.bfloat16)
 
         @pl.when(i < 7)
         def _():
-            source_free(i).start()
+            sums(i, 0).start()
 
         return carry
 
     lax.fori_loop(0, 8, backward, 0)
+
+    def rest(i, carry):
+        sums(i, 1).start()
+        return carry
+
+    lax.fori_loop(0, 7, rest, 0)
 
     for p in range(3):
         x_send(0, 0, p).wait_send()
@@ -233,13 +334,38 @@
     for k in range(2):
         c_send(0, far, k).wait_send()
 
-    total = sbuf[7].astype(jnp.float32)
-    for i in range(7):
-        source_free(i).wait_recv()
-        total += rbuf[i].astype(jnp.float32)
-    out_ref[...] = total.astype(jnp.bfloat16)
-    for i in range(7):
-        source_free(i).wait_send()
+    for k in range(NY):
+        move_send(k).wait_send()
+    grads_swap.wait_send()
+
+    def give(ref, work, received):
+        for at in range(MOVE // UNIT):
+            for first, rows, index in ((BASE, work, at), (CAP, received, MOVE // UNIT - 1 - at)):
+                here = first + at * UNIT
+                if rows is not None:
+                    mask = own_live[here : here + UNIT]
+                    ref[pl.ds(here, UNIT)] = pick(mask, rows[pl.ds(index * UNIT, UNIT)], None)
+
+    att_ref[pl.ds(0, BASE)] = attw[pl.ds(0, BASE)]
+    att_swap.wait()
+    give(att_ref, attw.at[pl.ds(BASE, MOVE)], am)
+
+    def added(b):
+        total = sbuf[7, parts[b]].astype(jnp.float32)
+        for i in range(7):
+            sums(i, b).wait_recv()
+            total += rbuf[i, parts[b]].astype(jnp.float32)
+        return total.astype(jnp.bfloat16)
+
+    outw[...] = added(0)
+    out_swap.start()
+    give(out_ref, outw, None)
+    out_ref[pl.ds(0, BASE)] = added(1)
+    out_swap.wait()
+    give(out_ref, None, om)
+    for b in range(2):
+        for i in range(7):
+            sums(i, b).wait_send()
 
 
 def local(patches, qkv_weight, out_grad, image_starts):
@@ -247,7 +373,6 @@
     share = qkv_weight.shape[0]
     columns = qkv_weight.shape[1] * qkv_weight.shape[2]
     n_dp = model // share
-    ids = lax.dynamic_index_in_dim(image_starts, lax.axis_index("dp"), 0, keepdims=False)
     vmem = pl.BlockSpec(memory_space=pltpu.VMEM)
     bf = jnp.bfloat16
     dma = pltpu.SemaphoreType.DMA
@@ -258,28 +383,41 @@
             jax.ShapeDtypeStruct(out_grad.shape, bf),
             jax.ShapeDtypeStruct((rows, model // 8), bf),
         ),
-        in_specs=[vmem] * 5,
+        in_specs=[pl.BlockSpec(memory_space=pl.ANY), vmem, vmem, vmem],
         out_specs=(vmem, vmem),
         scratch_shapes=[
-            pltpu.VMEM((n_dp, share, columns), bf),
-            pltpu.VMEM((rows, columns), jnp.float32),
-            pltpu.VMEM((rows, columns), bf),
-            pltpu.VMEM((rows, columns), bf),
-            pltpu.VMEM((8, rows, model // 8), bf),
-            pltpu.VMEM((7, rows, model // 8), bf),
+            pltpu.VMEM((n_dp, 3, share, columns // 3), bf),
+            pltpu.VMEM((CAP, columns), jnp.float32),
+            pltpu.VMEM((CAP, columns), bf),
+            pltpu.VMEM((CAP, columns), bf),
+            pltpu.VMEM((8, CAP, model // 8), bf),
+            pltpu.VMEM((7, CAP, model // 8), bf),
+            pltpu.VMEM((CAP, model), bf),
+            pltpu.VMEM((NY, MOVE, model // NY), bf),
+            pltpu.VMEM((CAP, columns // 3), bf),
+            pltpu.VMEM((MOVE, columns // 3), bf),
+            pltpu.VMEM((CAP, columns // 3), bf),
+            pltpu.VMEM((MOVE, columns // 3), bf),
+            pltpu.VMEM((MOVE, model // 8), bf),
+            pltpu.VMEM((MOVE, model // 8), bf),
             dma((2, steps, 4)),
             dma((2, steps, 4)),
             dma((2, steps, 3)),
             dma((2, steps, 3)),
             dma((2, steps, 2)),
             dma((2, steps, 2)),
-            dma((8,)),
-            dma((8,)),
+            dma((2, 8)),
+            dma((2, 8)),
+            dma((NY,)),
+            dma((NY,)),
+            dma((3,)),
+            dma((3,)),
+            dma(()),
         ],
         compiler_params=pltpu.CompilerParams(
             collective_id=0, has_side_effects=True, vmem_limit_bytes=56 * 1024 * 1024
         ),
-    )(patches, qkv_weight.reshape(share, columns), out_grad, ids[:, None], ids[None, :])
+    )(patches, qkv_weight.transpose(1, 0, 2), out_grad, image_starts)
 
 
 def solution(mesh):

time: 124 us -> 109 us (0.88)
  Pallas kernels: 116 us -> 105 us
  local copies, waits for them, and re-layouts: 7.18 us -> 3.33 us
    pallas_call x1, Pallas kernels: 116 us -> 105 us  [local(): pl.pallas_call(kernel, out_shape=(jax.ShapeDtypeStruct(out_grad.shape, bf...]
    reshape x1 -> x0, local copies, waits for them, and re-layouts: 1.64 us -> none  [local(): qkv_weight.reshape(share, columns)]
    unnamed x4 -> x2, local copies, waits for them, and re-layouts: 4.17 us -> 3.33 us
where the time goes in v2:
time: 109 us
  Pallas kernels  105 us (96%)
  local copies, waits for them, and re-layouts  3.33 us (3%)
    pallas_call x1, Pallas kernels, local(): pl.pallas_call(kernel, out_shape=(jax.ShapeDtypeStruct(out_grad.shape, bf...  105 us
    unnamed x2, local copies, waits for them, and re-layouts  3.33 us

profile of v2, /device:TPU:1, one launch (start us, length us, event | category | flops | bytes accessed | tf_op | source)
XLA Modules:
  0.0 108.6 jit_solution(1389791233793116593)
XLA Ops:
  0.6 104.6 %shard_map.59 = (bf16[224,384]{1,0:T(8,128)(2,1)}, bf16[224,768]{1,0:T(8,128)(2,1)}) custom-call(bf16[224,6144]{1,0:T(8,128)(2,1)} %x_ref.1, bf16[3,96,384]{2,1,0:T(8,128)(2,1)} %bitcast.1, bf16[224,384]{1,0:T(8,128)(2,1)} %g_ref.1, s32[64,224]{1,0:T(8,128)} %ids_ref.1), custom_call_target="tpu_custom_call" | custom-call | tf_op jit(solution)/shard_map/pallas_call | solution.py:380
  105.2 1.6 %copy.8 = bf16[224,384]{1,0:T(8,128)(2,1)} copy(bf16[224,384]{1,0:T(8,128)(2,1)} %get-tuple-element.4) | data formatting | bytes 344064
  106.8 1.7 %copy.9 = bf16[224,768]{1,0:T(8,128)(2,1)} copy(bf16[224,768]{1,0:T(8,128)(2,1)} %get-tuple-element.5) | data formatting | bytes 688128

commit v3 on v2

--- a/solution.py
+++ b/solution.py
@@ -14,6 +14,7 @@
 CAP = 160
 MOVE = 64
 BASE = CAP - MOVE
+EARLY = 32
 MESH = pl.DeviceIdType.MESH
 
 
@@ -53,14 +54,14 @@
 
 def kernel(
     x_ref, w_ref, g_ref, ids_ref, att_ref, out_ref,
-    wbuf, acc, qkv, gbuf, sbuf, rbuf, xw, mbuf, gw, gm, attw, am, outw, om,
-    zs, zr, xs, xr, cs, cr, ts, tr, ms, mr, ps, pr, lsem,
+    wbuf, acc, qkv, gbuf, sbuf, rbuf, xw, mbuf, wrem, grem, gs, gw, gm, attw, am, ats, arem, outw, om,
+    zs, zr, xs, xr, cs, cr, ts, tr, ms, mr, ps, pr, bs, br, lsem,
 ):
     dp, t = lax.axis_index("dp"), lax.axis_index("tensor")
     xl, z, c = dp // (2 * NZ), (dp // 2) % NZ, dp % 2
     y, xh = t // 2, t % 2
     share, width = w_ref.shape[1:]
-    slot = g_ref.shape[0]
+    b_own = dp
     quarter = xw.shape[1] // NY
     heads = width // HD
 
@@ -71,6 +72,7 @@
     x_dev = dev(1 - xl, z, c)
     c_dev = dev(xl, z, 1 - c)
     cross = (dev(1 - xl, z, c)[0], y * 2 + 1 - xh)
+    sib = (dp, y * 2 + 1 - xh)
     peers = [(dp, ((y + j // 2) % NY) * 2 + (xh + j) % 2) for j in range(1, 8)]
 
     barrier = pltpu.get_barrier_semaphore()
@@ -82,14 +84,20 @@
     def origin(d, s):
         return (z - s + NZ) % NZ if d == 0 else (z + s) % NZ
 
-    def part(xl_, z_, c_, p):
-        return wbuf.at[xl_ * (2 * NZ) + z_ * 2 + c_, p]
+    def block(xl_, z_, c_):
+        return xl_ * (2 * NZ) + z_ * 2 + c_
+
+    def x_ref_part(xl_, zo, p):
+        at = block(xl_, zo, c)
+        if p == 0:
+            return wbuf.at[at, 0, :, pl.ds(EARLY, share - EARLY), :]
+        return wbuf.at[at, 0, :, pl.ds(0, EARLY), :] if p == 3 else wbuf.at[at, p]
 
     def whole(xl_, z_, c_):
-        return wbuf.at[xl_ * (2 * NZ) + z_ * 2 + c_]
+        return wbuf.at[block(xl_, z_, c_)]
 
     def z_ref(zo, p):
-        return part(1 - xl, zo, c, 0) if p == 0 else part(xl, zo, c, p - 1)
+        return x_ref_part(1 - xl, zo, 3) if p == 0 else wbuf.at[block(xl, zo, c), p - 1]
 
     def remote(ref, send, recv, device):
         return pltpu.make_async_remote_copy(
@@ -103,10 +111,10 @@
         return remote(z_ref(origin(d, s), p), zs.at[d, s, p], zr.at[d, s, p], z_next[d])
 
     def x_send(d, s, p):
-        return remote(part(xl, origin(d, s), c, p), xs.at[d, s, p], xr.at[d, s, p], x_dev)
+        return remote(x_ref_part(xl, origin(d, s), p), xs.at[d, s, p], xr.at[d, s, p], cross if p == 2 else x_dev)
 
     def x_recv(d, s, p):
-        return remote(part(1 - xl, origin(d, s), c, p), xs.at[d, s, p], xr.at[d, s, p], x_dev)
+        return remote(x_ref_part(1 - xl, origin(d, s), p), xs.at[d, s, p], xr.at[d, s, p], cross if p == 2 else x_dev)
 
     def c_send(d, s, k):
         return remote(whole((xl + k) % 2, origin(d, s), c), cs.at[d, s, k], cr.at[d, s, k], c_dev)
@@ -116,7 +124,12 @@
 
     def weight_rows(first, count):
         return jnp.concatenate(
-            [wbuf[pl.ds(first, count), p].reshape(count * share, width) for p in range(3)], axis=1
+            [
+                wbuf[pl.ds(first, count), j, i].reshape(count * share, HD)
+                for i in range(3)
+                for j in range(heads)
+            ],
+            axis=1,
         )
 
     def multiply(s):
@@ -140,24 +153,80 @@
     def move_recv(k):
         return move_copy(k, (y - k + NY) % NY, cross)
 
-    def swap(k, src, dst):
+    def swap(k, src, dst, device):
         return pltpu.make_async_remote_copy(
-            src_ref=src, dst_ref=dst, send_sem=ps.at[k], recv_sem=pr.at[k], device_id=x_dev, device_id_type=MESH
-        )
-
-    grads_swap = swap(0, g_ref.at[pl.ds(CAP, MOVE)], gm)
-    att_swap = swap(1, attw.at[pl.ds(BASE, MOVE)], am)
-    out_swap = swap(2, outw, om)
+            src_ref=src, dst_ref=dst, send_sem=ps.at[k], recv_sem=pr.at[k], device_id=device, device_id_type=MESH
+        )
+
+    def with_sib(k, src, dst):
+        return pltpu.make_async_remote_copy(
+            src_ref=src, dst_ref=dst, send_sem=bs.at[k], recv_sem=br.at[k], device_id=sib, device_id_type=MESH
+        )
+
+    pair, lone = pl.ds(0, 2), pl.ds(2, 1)
+    moved, tail = pl.ds(CAP, MOVE), pl.ds(BASE, MOVE)
+    grads_swaps = (
+        swap(0, gs.at[pair, moved], gm.at[pair], x_dev),
+        swap(1, gs.at[lone, moved], gm.at[lone], cross),
+    )
+    att_swaps = (
+        swap(2, attw.at[pair, tail], am.at[pair], x_dev),
+        swap(3, attw.at[lone, tail], am.at[lone], cross),
+    )
+    out_swap = swap(4, outw, om, x_dev)
+    weight_sib = with_sib(0, wrem, wbuf.at[b_own, 2])
+    grads_sib = with_sib(1, grem, gs.at[2])
+    att_sib = with_sib(2, ats.at[2], arem)
+
+    def head(k):
+        return pl.ds(pl.multiple_of(k * HD, HD), HD)
+
+    kept = (head(xh), head(xh + 1))
+    spare = head(2 - 2 * xh)
+    same = xl == 0
     own_rows = pltpu.make_async_copy(x_ref.at[pl.ds(0, CAP)], xw, lsem)
 
     own_rows.start()
-    wbuf[xl * (2 * NZ) + z * 2 + c] = w_ref[...]
-    for p in range(3):
+    for i in range(3):
+        wrem[i] = w_ref[i, :, spare]
+
+    @pl.when(xl == 1)
+    def _():
+        weight_sib.start()
+
+    for j in range(2):
+        for i in range(3):
+            wbuf[b_own, j, i] = w_ref[i, :, kept[j]]
+    for p in (3, 0, 1):
         x_send(0, 0, p).start()
-    for p in range(1, 4):
+    for p in (1, 2):
         for d in range(2):
             z_send(d, 1, p).start()
+
+    @pl.when(same)
+    def _():
+        wbuf[b_own, 2] = wrem[...]
+
+    grem[...] = g_ref[:, spare]
+    for j in range(2):
+        gs[j] = g_ref[:, kept[j]]
+
+    @pl.when(same)
+    def _():
+        gs[2] = grem[...]
+
+    @pl.when(xl == 1)
+    def _():
+        grads_sib.start()
+        weight_sib.wait_recv()
+
+    x_send(0, 0, 2).start()
+    for d in range(2):
+        z_send(d, 1, 3).start()
     c_send(0, 0, 0).start()
+    x_recv(0, 0, 3).wait_recv()
+    for d in range(2):
+        z_send(d, 1, 0).start()
     move_send(0).start()
     acc[...] = jnp.zeros_like(acc)
     own_ids = column(ids_ref, dp)
@@ -181,20 +250,17 @@
                 cols = pl.ds(q * quarter, quarter)
                 xw[rows, cols] = pick(mask, xw[rows, cols], mbuf[q, back, :])
 
-    x_recv(0, 0, 0).wait_recv()
-    for d in range(2):
-        z_send(d, 1, 0).start()
-    x_recv(0, 0, 1).wait_recv()
-    x_recv(0, 0, 2).wait_recv()
+    for p in range(3):
+        x_recv(0, 0, p).wait_recv()
     c_send(0, 0, 1).start()
 
-    order = (2, 3, 1, 0)
-    last = {0: 0, 1: 0, 2: 1, 3: 1}
+    order = (1, 2, 3, 0)
+    last = {1: 0, 2: 0, 3: 1, 0: 1}
     far = NZ // 2
 
     def pass_x(d, s):
-        x_recv(d, s, 1).wait_recv()
-        x_recv(d, s, 2).wait_recv()
+        for p in range(3):
+            x_recv(d, s, p).wait_recv()
         c_send(d, s, 1).start()
 
     def use(ds, s):
@@ -213,7 +279,7 @@
                     @pl.when(s < far - 1)
                     def _():
                         z_send(d, s + 1, p).start()
-                if p >= 2:
+                if p >= 1:
                     x_send(d, s, p - 1).start()
         for d in range(2):
             c_send(d, s, 0).start()
@@ -225,7 +291,13 @@
             move_recv(0).wait_recv()
             for k in range(1, NY):
                 move_send(k).start()
-            grads_swap.start()
+
+            @pl.when(xl == 1)
+            def _():
+                grads_sib.wait_recv()
+
+            for copy in grads_swaps:
+                copy.start()
 
         @pl.when(s > 1)
         def _():
@@ -245,7 +317,7 @@
     lax.fori_loop(1, far, step, 0)
     for p in order:
         z_recv(last[p], far, p).wait_recv()
-        if p >= 2:
+        if p >= 1:
             x_send(0, far, p - 1).start()
     c_send(0, far, 0).start()
     for d in range(2):
@@ -259,22 +331,25 @@
     row_ids = work_ids.T[:1]
     allowed = (work_ids[:, :1] == row_ids) & (row_ids >= 0.0)
     live = (work_ids[:, :1] >= 0.0).astype(jnp.float32)
-    grads_swap.wait_recv()
-    gw[pl.ds(0, BASE)] = g_ref[pl.ds(0, BASE)]
-    for at in range(MOVE // UNIT):
-        rows = pl.ds(BASE + at * UNIT, UNIT)
-        mask = own_live[BASE + at * UNIT : BASE + (at + 1) * UNIT]
-        gw[rows] = pick(mask, g_ref[rows], gm[pl.ds(MOVE - (at + 1) * UNIT, UNIT)])
+    for copy in grads_swaps:
+        copy.wait_recv()
+    for j in range(heads):
+        gw[j, pl.ds(0, BASE)] = gs[j, pl.ds(0, BASE)]
+        for at in range(MOVE // UNIT):
+            rows = pl.ds(BASE + at * UNIT, UNIT)
+            mask = own_live[BASE + at * UNIT : BASE + (at + 1) * UNIT]
+            gw[j, rows] = pick(mask, gs[j, rows], gm[j, pl.ds(MOVE - (at + 1) * UNIT, UNIT)])
     for h in range(heads):
         at = [slice(i * width + h * HD, i * width + (h + 1) * HD) for i in range(3)]
         attended, *grads = attend_head(
-            qkv[:, at[0]], qkv[:, at[1]], qkv[:, at[2]], gw[:, h * HD : (h + 1) * HD], allowed, live
-        )
-        attw[:, h * HD : (h + 1) * HD] = attended
+            qkv[:, at[0]], qkv[:, at[1]], qkv[:, at[2]], gw[h], allowed, live
+        )
+        attw[h] = attended
         for i in range(3):
             gbuf[:, at[i]] = grads[i]
 
-    att_swap.start()
+    for copy in att_swaps:
+        copy.start()
 
     blocks = wbuf.shape[0] // 8
 
@@ -311,7 +386,7 @@
 
     lax.fori_loop(0, 7, rest, 0)
 
-    for p in range(3):
+    for p in range(4):
         x_send(0, 0, p).wait_send()
     for k in range(2):
         c_send(0, 0, k).wait_send()
@@ -320,7 +395,7 @@
         for d in range(2):
             for p in range(4):
                 z_send(d, s, p).wait_send()
-            for p in (1, 2):
+            for p in range(3):
                 x_send(d, s, p).wait_send()
             for k in range(2):
                 c_send(d, s, k).wait_send()
@@ -329,14 +404,15 @@
     lax.fori_loop(1, NZ // 2, drain, 0)
     for p in range(4):
         z_send(last[p], far, p).wait_send()
-    for p in (1, 2):
+    for p in range(3):
         x_send(0, far, p).wait_send()
     for k in range(2):
         c_send(0, far, k).wait_send()
 
     for k in range(NY):
         move_send(k).wait_send()
-    grads_swap.wait_send()
+    for copy in grads_swaps:
+        copy.wait_send()
 
     def give(ref, work, received):
         for at in range(MOVE // UNIT):
@@ -346,9 +422,24 @@
                     mask = own_live[here : here + UNIT]
                     ref[pl.ds(here, UNIT)] = pick(mask, rows[pl.ds(index * UNIT, UNIT)], None)
 
-    att_ref[pl.ds(0, BASE)] = attw[pl.ds(0, BASE)]
-    att_swap.wait()
-    give(att_ref, attw.at[pl.ds(BASE, MOVE)], am)
+    for copy in att_swaps:
+        copy.wait()
+    for j in range(heads):
+        ats[j, pl.ds(0, BASE)] = attw[j, pl.ds(0, BASE)]
+        give(ats.at[j], attw.at[j, tail], am.at[j])
+
+    @pl.when(xl == 1)
+    def _():
+        att_sib.start()
+        weight_sib.wait_send()
+        grads_sib.wait_send()
+
+    for j in range(2):
+        att_ref[:, kept[j]] = ats[j]
+
+    @pl.when(same)
+    def _():
+        att_ref[:, spare] = ats[2]
 
     def added(b):
         total = sbuf[7, parts[b]].astype(jnp.float32)
@@ -359,6 +450,12 @@
 
     outw[...] = added(0)
     out_swap.start()
+
+    @pl.when(xl == 1)
+    def _():
+        att_sib.wait()
+        att_ref[:, spare] = arem[...]
+
     give(out_ref, outw, None)
     out_ref[pl.ds(0, BASE)] = added(1)
     out_swap.wait()
@@ -373,6 +470,7 @@
     share = qkv_weight.shape[0]
     columns = qkv_weight.shape[1] * qkv_weight.shape[2]
     n_dp = model // share
+    heads = columns // (3 * HD)
     vmem = pl.BlockSpec(memory_space=pltpu.VMEM)
     bf = jnp.bfloat16
     dma = pltpu.SemaphoreType.DMA
@@ -386,7 +484,7 @@
         in_specs=[pl.BlockSpec(memory_space=pl.ANY), vmem, vmem, vmem],
         out_specs=(vmem, vmem),
         scratch_shapes=[
-            pltpu.VMEM((n_dp, 3, share, columns // 3), bf),
+            pltpu.VMEM((n_dp, heads, 3, share, HD), bf),
             pltpu.VMEM((CAP, columns), jnp.float32),
             pltpu.VMEM((CAP, columns), bf),
             pltpu.VMEM((CAP, columns), bf),
@@ -394,22 +492,29 @@
             pltpu.VMEM((7, CAP, model // 8), bf),
             pltpu.VMEM((CAP, model), bf),
             pltpu.VMEM((NY, MOVE, model // NY), bf),
-            pltpu.VMEM((CAP, columns // 3), bf),
-            pltpu.VMEM((MOVE, columns // 3), bf),
-            pltpu.VMEM((CAP, columns // 3), bf),
-            pltpu.VMEM((MOVE, columns // 3), bf),
+            pltpu.VMEM((3, share, HD), bf),
+            pltpu.VMEM((rows, HD), bf),
+            pltpu.VMEM((heads, rows, HD), bf),
+            pltpu.VMEM((heads, CAP, HD), bf),
+            pltpu.VMEM((heads, MOVE, HD), bf),
+            pltpu.VMEM((heads, CAP, HD), bf),
+            pltpu.VMEM((heads, MOVE, HD), bf),
+            pltpu.VMEM((heads, rows, HD), bf),
+            pltpu.VMEM((rows, HD), bf),
             pltpu.VMEM((MOVE, model // 8), bf),
             pltpu.VMEM((MOVE, model // 8), bf),
             dma((2, steps, 4)),
             dma((2, steps, 4)),
-            dma((2, steps, 3)),
-            dma((2, steps, 3)),
+            dma((2, steps, 4)),
+            dma((2, steps, 4)),
             dma((2, steps, 2)),
             dma((2, steps, 2)),
             dma((2, 8)),
             dma((2, 8)),
             dma((NY,)),
             dma((NY,)),
+            dma((5,)),
+            dma((5,)),
             dma((3,)),
             dma((3,)),
             dma(()),

time: 109 us -> 104 us (0.954)
  Pallas kernels: 105 us -> 99.6 us
    pallas_call x1, Pallas kernels: 105 us -> 99.6 us  [local(): pl.pallas_call(kernel, out_shape=(jax.ShapeDtypeStruct(out_grad.shape, bf...]
where the time goes in v3:
time: 104 us
  Pallas kernels  99.6 us (96%)
  local copies, waits for them, and re-layouts  3.33 us (3%)
    pallas_call x1, Pallas kernels, local(): pl.pallas_call(kernel, out_shape=(jax.ShapeDtypeStruct(out_grad.shape, bf...  99.6 us
    unnamed x2, local copies, waits for them, and re-layouts  3.33 us

profile of v3, /device:TPU:1, one launch (start us, length us, event | category | flops | bytes accessed | tf_op | source)
XLA Modules:
  0.0 103.6 jit_solution(8588120695853563151)
XLA Ops:
  0.6 99.6 %shard_map.59 = (bf16[224,384]{1,0:T(8,128)(2,1)}, bf16[224,768]{1,0:T(8,128)(2,1)}) custom-call(bf16[224,6144]{1,0:T(8,128)(2,1)} %x_ref.1, bf16[3,96,384]{2,1,0:T(8,128)(2,1)} %bitcast.1, bf16[224,384]{1,0:T(8,128)(2,1)} %g_ref.1, s32[64,224]{1,0:T(8,128)} %ids_ref.1), custom_call_target="tpu_custom_call" | custom-call | tf_op jit(solution)/shard_map/pallas_call | solution.py:478
  100.3 1.6 %copy.8 = bf16[224,384]{1,0:T(8,128)(2,1)} copy(bf16[224,384]{1,0:T(8,128)(2,1)} %get-tuple-element.4) | data formatting | bytes 344064
  101.9 1.7 %copy.9 = bf16[224,768]{1,0:T(8,128)(2,1)} copy(bf16[224,768]{1,0:T(8,128)(2,1)} %get-tuple-element.5) | data formatting | bytes 688128

commit v4 on v3

--- a/solution.py
+++ b/solution.py
@@ -15,6 +15,7 @@
 MOVE = 64
 BASE = CAP - MOVE
 EARLY = 32
+FILL = 5
 MESH = pl.DeviceIdType.MESH
 
 
@@ -79,7 +80,6 @@
     everyone = [*z_next, x_dev, c_dev, cross, *peers]
     for other in everyone:
         pl.semaphore_signal(barrier, inc=1, device_id=other, device_id_type=MESH)
-    pl.semaphore_wait(barrier, len(everyone))
 
     def origin(d, s):
         return (z - s + NZ) % NZ if d == 0 else (z + s) % NZ
@@ -189,19 +189,9 @@
     own_rows.start()
     for i in range(3):
         wrem[i] = w_ref[i, :, spare]
-
-    @pl.when(xl == 1)
-    def _():
-        weight_sib.start()
-
     for j in range(2):
         for i in range(3):
             wbuf[b_own, j, i] = w_ref[i, :, kept[j]]
-    for p in (3, 0, 1):
-        x_send(0, 0, p).start()
-    for p in (1, 2):
-        for d in range(2):
-            z_send(d, 1, p).start()
 
     @pl.when(same)
     def _():
@@ -215,19 +205,6 @@
     def _():
         gs[2] = grem[...]
 
-    @pl.when(xl == 1)
-    def _():
-        grads_sib.start()
-        weight_sib.wait_recv()
-
-    x_send(0, 0, 2).start()
-    for d in range(2):
-        z_send(d, 1, 3).start()
-    c_send(0, 0, 0).start()
-    x_recv(0, 0, 3).wait_recv()
-    for d in range(2):
-        z_send(d, 1, 0).start()
-    move_send(0).start()
     acc[...] = jnp.zeros_like(acc)
     own_ids = column(ids_ref, dp)
     other_ids = column(ids_ref, dev(1 - xl, z, c)[0])
@@ -237,6 +214,31 @@
         for own, other in zip(units(own_ids, BASE), units(other_ids, CAP)[::-1], strict=True)
     ]
     work_ids = jnp.concatenate([own_ids[:BASE], *taken], axis=0)
+    pl.semaphore_wait(barrier, len(everyone))
+
+    @pl.when(xl == 1)
+    def _():
+        weight_sib.start()
+
+    for p in (3, 0, 1):
+        x_send(0, 0, p).start()
+    for p in (1, 2):
+        for d in range(2):
+            z_send(d, 1, p).start()
+
+    @pl.when(xl == 1)
+    def _():
+        grads_sib.start()
+        weight_sib.wait_recv()
+
+    x_send(0, 0, 2).start()
+    for d in range(2):
+        z_send(d, 1, 3).start()
+    c_send(0, 0, 0).start()
+    x_recv(0, 0, 3).wait_recv()
+    for d in range(2):
+        z_send(d, 1, 0).start()
+    move_send(0).start()
 
     def fill():
         for k in range(1, NY):
@@ -250,10 +252,6 @@
                 cols = pl.ds(q * quarter, quarter)
                 xw[rows, cols] = pick(mask, xw[rows, cols], mbuf[q, back, :])
 
-    for p in range(3):
-        x_recv(0, 0, p).wait_recv()
-    c_send(0, 0, 1).start()
-
     order = (1, 2, 3, 0)
     last = {1: 0, 2: 0, 3: 1, 0: 1}
     far = NZ // 2
@@ -263,11 +261,10 @@
             x_recv(d, s, p).wait_recv()
         c_send(d, s, 1).start()
 
-    def use(ds, s):
+    def landed(ds, s):
         for d in ds:
             for k in range(2):
                 c_recv(d, s, k).wait_recv()
-        multiply(s)
 
     def step(s, carry):
         for p in order:
@@ -286,8 +283,11 @@
 
         @pl.when(s == 1)
         def _():
-            for k in range(2):
-                c_recv(0, 0, k).wait_recv()
+            pass_x(0, 0)
+
+        @pl.when(s == 2)
+        def _():
+            landed((0,), 0)
             move_recv(0).wait_recv()
             for k in range(1, NY):
                 move_send(k).start()
@@ -304,13 +304,21 @@
             for d in range(2):
                 pass_x(d, s - 1)
 
-        @pl.when(s == 3)
+        @pl.when(s > 2)
+        def _():
+            landed((0, 1), s - 2)
+
+        @pl.when(s == FILL)
         def _():
             fill()
 
-        @pl.when(s > 2)
-        def _():
-            use((0, 1), s - 2)
+        @pl.when(s >= FILL)
+        def _():
+            multiply(2 * (s - FILL) + 1)
+
+        @pl.when((s >= FILL) & (s < far - 1))
+        def _():
+            multiply(2 * (s - FILL) + 2)
 
         return carry
 
@@ -322,10 +330,13 @@
     c_send(0, far, 0).start()
     for d in range(2):
         pass_x(d, far - 1)
-    use((0, 1), far - 2)
+    landed((0, 1), far - 2)
+    multiply(far - 2)
     pass_x(0, far)
-    use((0, 1), far - 1)
-    use((0,), far)
+    landed((0, 1), far - 1)
+    multiply(far - 1)
+    landed((0,), far)
+    multiply(far)
 
     qkv[...] = acc[...].astype(jnp.bfloat16)
     row_ids = work_ids.T[:1]

time: 104 us -> 102 us (0.981)
  Pallas kernels: 99.6 us -> 97.2 us
    pallas_call x1, Pallas kernels: 99.6 us -> 97.2 us  [local(): pl.pallas_call(kernel, out_shape=(jax.ShapeDtypeStruct(out_grad.shape, bf...]
where the time goes in v4:
time: 102 us; the launch traced here: 101 us
  Pallas kernels  97.2 us (95%)
  local copies, waits for them, and re-layouts  3.33 us (3%)
    pallas_call x1, Pallas kernels, local(): pl.pallas_call(kernel, out_shape=(jax.ShapeDtypeStruct(out_grad.shape, bf...  97.2 us
    unnamed x2, local copies, waits for them, and re-layouts  3.33 us

profile of v4, /device:TPU:1, one launch (start us, length us, event | category | flops | bytes accessed | tf_op | source)
XLA Modules:
  0.0 101.2 jit_solution(17338635537036273134)
XLA Ops:
  0.6 97.2 %shard_map.59 = (bf16[224,384]{1,0:T(8,128)(2,1)}, bf16[224,768]{1,0:T(8,128)(2,1)}) custom-call(bf16[224,6144]{1,0:T(8,128)(2,1)} %x_ref.1, bf16[3,96,384]{2,1,0:T(8,128)(2,1)} %bitcast.1, bf16[224,384]{1,0:T(8,128)(2,1)} %g_ref.1, s32[64,224]{1,0:T(8,128)} %ids_ref.1), custom_call_target="tpu_custom_call" | custom-call | tf_op jit(solution)/shard_map/pallas_call | solution.py:489
  97.8 1.6 %copy.8 = bf16[224,384]{1,0:T(8,128)(2,1)} copy(bf16[224,384]{1,0:T(8,128)(2,1)} %get-tuple-element.4) | data formatting | bytes 344064
  99.4 1.7 %copy.9 = bf16[224,768]{1,0:T(8,128)(2,1)} copy(bf16[224,768]{1,0:T(8,128)(2,1)} %get-tuple-element.5) | data formatting | bytes 688128

commit v5 on v4

--- a/solution.py
+++ b/solution.py
@@ -476,6 +476,21 @@
             sums(i, b).wait_send()
 
 
+def deliver_kernel(a_ref, b_ref, c_ref, d_ref):
+    c_ref[...] = a_ref[...]
+    d_ref[...] = b_ref[...]
+
+
+def deliver(*arrays):
+    vmem = pl.BlockSpec(memory_space=pltpu.VMEM)
+    return pl.pallas_call(
+        deliver_kernel,
+        out_shape=tuple(jax.ShapeDtypeStruct(a.shape, a.dtype) for a in arrays),
+        in_specs=[vmem] * 2,
+        out_specs=(vmem, vmem),
+    )(*arrays)
+
+
 def local(patches, qkv_weight, out_grad, image_starts):
     rows, model = patches.shape
     share = qkv_weight.shape[0]
@@ -486,7 +501,7 @@
     bf = jnp.bfloat16
     dma = pltpu.SemaphoreType.DMA
     steps = NZ // 2 + 1
-    return pl.pallas_call(
+    attended, patch_grad = pl.pallas_call(
         kernel,
         out_shape=(
             jax.ShapeDtypeStruct(out_grad.shape, bf),
@@ -534,6 +549,7 @@
             collective_id=0, has_side_effects=True, vmem_limit_bytes=56 * 1024 * 1024
         ),
     )(patches, qkv_weight.transpose(1, 0, 2), out_grad, image_starts)
+    return deliver(attended, patch_grad)
 
 
 def solution(mesh):

time: 102 us -> 100 us (0.980)
  local copies, waits for them, and re-layouts: 3.33 us -> 0 us
  Pallas kernels: 97.2 us -> 99.1 us
    unnamed x2 -> x0, local copies, waits for them, and re-layouts: 3.33 us -> none
    pallas_call x0 -> x1, Pallas kernels: none -> 1.88 us  [deliver(): pl.pallas_call(deliver_kernel, out_shape=tuple((jax.ShapeDtypeStruct(a.sh...]
where the time goes in v5:
time: 100 us; the launch traced here: 99.7 us
  Pallas kernels  99.1 us (99%)
    pallas_call x1, Pallas kernels, local(): pl.pallas_call(kernel, out_shape=(jax.ShapeDtypeStruct(out_grad.shape, bf...  97.2 us

profile of v5, /device:TPU:1, one launch (start us, length us, event | category | flops | bytes accessed | tf_op | source)
XLA Modules:
  0.0 99.7 jit_solution(5972110281681566891)
XLA Ops:
  0.6 97.2 %shard_map.59 = (bf16[224,384]{1,0:T(8,128)(2,1)}, bf16[224,768]{1,0:T(8,128)(2,1)}) custom-call(bf16[224,6144]{1,0:T(8,128)(2,1)} %x_ref.1, bf16[3,96,384]{2,1,0:T(8,128)(2,1)} %bitcast.1, bf16[224,384]{1,0:T(8,128)(2,1)} %g_ref.1, s32[64,224]{1,0:T(8,128)} %ids_ref.1), custom_call_target="tpu_custom_call" | custom-call | tf_op jit(solution)/shard_map/pallas_call | solution.py:504
  97.8 1.9 %shard_map.60 = (bf16[224,384]{1,0:T(8,128)(2,1)}, bf16[224,768]{1,0:T(8,128)(2,1)}) custom-call(bf16[224,384]{1,0:T(8,128)(2,1)} %get-tuple-element.4.a_ref, bf16[224,768]{1,0:T(8,128)(2,1)} %get-tuple-element.5.b_ref), custom_call_target="tpu_custom_call" | custom-call | tf_op jit(solution)/shard_map/pallas_call | solution.py:486

commit v6 on v5

--- a/solution.py
+++ b/solution.py
@@ -253,7 +253,7 @@
                 xw[rows, cols] = pick(mask, xw[rows, cols], mbuf[q, back, :])
 
     order = (1, 2, 3, 0)
-    last = {1: 0, 2: 0, 3: 1, 0: 1}
+    last = {1: 0, 2: 1, 3: 1, 0: 0}
     far = NZ // 2
 
     def pass_x(d, s):
@@ -366,7 +366,7 @@
 
     def dest(i):
         k = i // 2
-        dy = jnp.where(k < 2, k + 2, 3 - k)
+        dy = jnp.where(k < 2, 2 * k + 1, jnp.where(k == 2, 2, 0))
         return ((y + dy) % NY) * 2 + (xh + 1 - i % 2) % 2
 
     parts = (pl.ds(BASE, MOVE), pl.ds(0, BASE))

time: 100 us -> 99.7 us (level)
  no operation moved by 1% of the time
where the time goes in v6:
time: 99.7 us; the launch traced here: 99.5 us
  Pallas kernels  98.9 us (99%)
    pallas_call x1, Pallas kernels, local(): pl.pallas_call(kernel, out_shape=(jax.ShapeDtypeStruct(out_grad.shape, bf...  97 us

profile of v6, /device:TPU:1, one launch (start us, length us, event | category | flops | bytes accessed | tf_op | source)
XLA Modules:
  0.0 99.5 jit_solution(8609620664865150874)
XLA Ops:
  0.6 97.0 %shard_map.59 = (bf16[224,384]{1,0:T(8,128)(2,1)}, bf16[224,768]{1,0:T(8,128)(2,1)}) custom-call(bf16[224,6144]{1,0:T(8,128)(2,1)} %x_ref.1, bf16[3,96,384]{2,1,0:T(8,128)(2,1)} %bitcast.1, bf16[224,384]{1,0:T(8,128)(2,1)} %g_ref.1, s32[64,224]{1,0:T(8,128)} %ids_ref.1), custom_call_target="tpu_custom_call" | custom-call | tf_op jit(solution)/shard_map/pallas_call | solution.py:504
  97.6 1.9 %shard_map.60 = (bf16[224,384]{1,0:T(8,128)(2,1)}, bf16[224,768]{1,0:T(8,128)(2,1)}) custom-call(bf16[224,384]{1,0:T(8,128)(2,1)} %get-tuple-element.4.a_ref, bf16[224,768]{1,0:T(8,128)(2,1)} %get-tuple-element.5.b_ref), custom_call_target="tpu_custom_call" | custom-call | tf_op jit(solution)/shard_map/pallas_call | solution.py:486

commit v7 on v6

--- a/solution.py
+++ b/solution.py
@@ -369,7 +369,7 @@
         dy = jnp.where(k < 2, 2 * k + 1, jnp.where(k == 2, 2, 0))
         return ((y + dy) % NY) * 2 + (xh + 1 - i % 2) % 2
 
-    parts = (pl.ds(BASE, MOVE), pl.ds(0, BASE))
+    parts = (pl.ds(BASE, MOVE), pl.ds(0, BASE // 2), pl.ds(BASE // 2, BASE // 2))
 
     def sums(i, b):
         return pltpu.make_async_remote_copy(
@@ -391,11 +391,13 @@
 
     lax.fori_loop(0, 8, backward, 0)
 
-    def rest(i, carry):
-        sums(i, 1).start()
-        return carry
-
-    lax.fori_loop(0, 7, rest, 0)
+    for b in (1, 2):
+
+        def rest(i, carry, b=b):
+            sums(i, b).start()
+            return carry
+
+        lax.fori_loop(0, 7, rest, 0)
 
     for p in range(4):
         x_send(0, 0, p).wait_send()
@@ -468,10 +470,11 @@
         att_ref[:, spare] = arem[...]
 
     give(out_ref, outw, None)
-    out_ref[pl.ds(0, BASE)] = added(1)
+    for b in (1, 2):
+        out_ref[parts[b]] = added(b)
     out_swap.wait()
     give(out_ref, None, om)
-    for b in range(2):
+    for b in range(3):
         for i in range(7):
             sums(i, b).wait_send()
 
@@ -535,8 +538,8 @@
             dma((2, steps, 4)),
             dma((2, steps, 2)),
             dma((2, steps, 2)),
-            dma((2, 8)),
-            dma((2, 8)),
+            dma((3, 8)),
+            dma((3, 8)),
             dma((NY,)),
             dma((NY,)),
             dma((5,)),

time: 99.7 us -> 99.7 us (level)
  no operation moved by 1% of the time
where the time goes in v7:
time: 99.7 us; the launch traced here: 99.5 us
  Pallas kernels  98.9 us (99%)
    pallas_call x1, Pallas kernels, local(): pl.pallas_call(kernel, out_shape=(jax.ShapeDtypeStruct(out_grad.shape, bf...  97 us

profile of v7, /device:TPU:1, one launch (start us, length us, event | category | flops | bytes accessed | tf_op | source)
XLA Modules:
  0.0 99.5 jit_solution(5214261184683983496)
XLA Ops:
  0.6 97.0 %shard_map.59 = (bf16[224,384]{1,0:T(8,128)(2,1)}, bf16[224,768]{1,0:T(8,128)(2,1)}) custom-call(bf16[224,6144]{1,0:T(8,128)(2,1)} %x_ref.1, bf16[3,96,384]{2,1,0:T(8,128)(2,1)} %bitcast.1, bf16[224,384]{1,0:T(8,128)(2,1)} %g_ref.1, s32[64,224]{1,0:T(8,128)} %ids_ref.1), custom_call_target="tpu_custom_call" | custom-call | tf_op jit(solution)/shard_map/pallas_call | solution.py:507
  97.7 1.9 %shard_map.60 = (bf16[224,384]{1,0:T(8,128)(2,1)}, bf16[224,768]{1,0:T(8,128)(2,1)}) custom-call(bf16[224,384]{1,0:T(8,128)(2,1)} %get-tuple-element.4.a_ref, bf16[224,768]{1,0:T(8,128)(2,1)} %get-tuple-element.5.b_ref), custom_call_target="tpu_custom_call" | custom-call | tf_op jit(solution)/shard_map/pallas_call | solution.py:489
